TPU v7x, 32 devices: a whole 2x2x4 slice. The times are simulated.
32 devices in a mesh: group: 1, tm: 16 (over z, y, core), head: 2 (over x), sub: 1.
Axes of the slice: x: 2, y: 2, z: 4, core: 2. Of those that a mesh axis runs over, the one named last changes fastest.
Arguments:
- queries: bfloat16 [4096, 3072], P(('group', 'tm'), ('head', 'sub')), may hold values from -12 to 12
- keys_in: bfloat16 [4096, 3072], P(('group', 'tm'), ('head', 'sub')), may hold values from -12 to 12
- values_in: bfloat16 [4096, 3072], P(('group', 'tm'), ('head', 'sub')), may hold values from -6 to 6
- out_grad: bfloat16 [4096, 3072], P(('group', 'tm'), ('head', 'sub')), may hold values from -6 to 6
- band_mask: int32 [32, 6], P('tm'), may hold values from 0 to 1, as said below
- far_tiles: int32 [16, 16], replicated, may hold values from 0 to 1
Outputs:
- attended: bfloat16 [4096, 3072], P(('group', 'tm'), ('head', 'sub'))
- query_grad: bfloat16 [4096, 3072], P(('group', 'tm'), ('head', 'sub'))
- key_grad: bfloat16 [4096, 3072], P(('group', 'tm'), ('head', 'sub'))
- value_grad: bfloat16 [4096, 3072], P(('group', 'tm'), ('head', 'sub'))
Inputs may be any that keep to these rules, and one draw needn't show every extreme that they name: `band_mask`: row t and column w refer to query tile t and window tile w of t's block; the entry of t's own tile is always 1. `far_tiles`: entries are read only where the two blocks lie a power of two from 1 up apart.
All inputs are finite; a program needn't handle non-finite values.
Results may differ from a plain program's by a relative error of at most 0.023.
Values may be sent and summed in bfloat16 or wider, within the bound.
A program may use at most 128 MiB of HBM per device.

v0:
```python
import math

import jax
import jax.numpy as jnp
from jax import lax
from jax.sharding import PartitionSpec as P

D_HEAD = 128
TILE = 128
HALO = 256


def extended(cells, sides, width):
    for axis, dim in sides:
        count = lax.axis_size(axis)
        ends = count - 1
        head = lax.slice_in_dim(cells, 0, width, axis=dim)
        tail = lax.slice_in_dim(cells, cells.shape[dim] - width, cells.shape[dim], axis=dim)
        cells = jnp.concatenate(
            [
                lax.ppermute(tail, axis, [(i, (i + 1) % count) for i in range(ends)]),
                cells,
                lax.ppermute(head, axis, [((i + 1) % count, i) for i in range(ends)]),
            ],
            axis=dim,
        )
    return cells


def from_behind(value, axis, steps):
    count = lax.axis_size(axis)
    leading, last = (max(0, -steps), min(count, count - steps))
    return lax.ppermute(value, axis, [(source, source + steps) for source in range(leading, last)])


def far_offsets(count):
    offsets = []
    for level in range(0, count.bit_length()):
        stride = 1 << level
        if stride < count:
            offsets = offsets + [stride, -stride]
    return offsets


def per_device(queries, keys_in, values_in, out_grad, band_mask, far_tiles):
    tok_rows, head_cols = queries.shape
    heads_local = head_cols // D_HEAD
    score_scale = 1.0 / math.sqrt(D_HEAD)
    block_count = lax.axis_size("tm")
    position = lax.axis_index("tm")
    offset_list = far_offsets(block_count)
    far_slots = len(offset_list)
    offsets = jnp.array(offset_list, dtype=jnp.int32)
    tile_count = tok_rows // TILE
    halo_tiles = HALO // TILE
    window_tiles = tile_count + 2 * halo_tiles
    window_rows = tok_rows + 2 * HALO
    pair_cols = 2 * head_cols
    key_value = jnp.concatenate([keys_in, values_in], axis=1)
    window = extended(key_value, (("tm", 0),), HALO)
    pieces = []
    for offset in offset_list:
        reader = jnp.clip(position + offset, 0, block_count - 1)
        chosen = lax.dynamic_slice(far_tiles, (reader, position), (1, 1))[0, 0]
        tile_rows = lax.dynamic_slice_in_dim(key_value, chosen * TILE, TILE, 0)
        pieces.append(from_behind(tile_rows, "tm", offset))
    far_block = jnp.concatenate(pieces, axis=0)
    key_set = jnp.concatenate([window, far_block], axis=0)
    source_ids = position - offsets
    source_live = (source_ids >= 0) & (source_ids < block_count)
    global_tiles = position * tile_count - halo_tiles + jnp.arange(window_tiles, dtype=jnp.int32)
    inside = (global_tiles >= 0) & (global_tiles < block_count * tile_count)
    tile_live = (band_mask != 0) & inside[None, :]
    full_live = jnp.concatenate(
        [tile_live, jnp.broadcast_to(source_live[None, :], (tile_count, far_slots))], axis=1
    )
    live_mask = jnp.repeat(jnp.repeat(full_live, TILE, axis=0), TILE, axis=1)
    out_parts, query_parts, key_parts, value_parts = ([], [], [], [])
    for head_idx in range(heads_local):
        low = head_idx * D_HEAD
        query_head = queries[:, low : low + D_HEAD]
        grad_head = out_grad[:, low : low + D_HEAD]
        key_head = key_set[:, low : low + D_HEAD]
        value_head = key_set[:, head_cols + low : head_cols + low + D_HEAD]
        scores = (
            jnp.einsum("qd,kd->qk", query_head, key_head, preferred_element_type=jnp.float32)
            * score_scale
        )
        scores = jnp.where(live_mask, scores, -1e30)
        top_score = jnp.max(scores, axis=-1, keepdims=True)
        raised = jnp.exp(scores - top_score)
        weights = raised / jnp.sum(raised, axis=-1, keepdims=True)
        weights_b = weights.astype(jnp.bfloat16)
        out_head = jnp.dot(weights_b, value_head, preferred_element_type=jnp.float32).astype(
            jnp.bfloat16
        )
        dweights = jnp.einsum(
            "qd,kd->qk", grad_head, value_head, preferred_element_type=jnp.float32
        )
        row_delta = jnp.sum(
            grad_head.astype(jnp.float32) * out_head.astype(jnp.float32), axis=-1, keepdims=True
        )
        dscores = (weights * (dweights - row_delta)).astype(jnp.bfloat16)
        query_part = jnp.dot(dscores, key_head, preferred_element_type=jnp.float32) * score_scale
        key_part = (
            jnp.einsum("qk,qd->kd", dscores, query_head, preferred_element_type=jnp.float32)
            * score_scale
        )
        value_part = jnp.einsum(
            "qk,qd->kd", weights_b, grad_head, preferred_element_type=jnp.float32
        )
        out_parts.append(out_head)
        query_parts.append(query_part.astype(jnp.bfloat16))
        key_parts.append(key_part)
        value_parts.append(value_part)
    attended = jnp.concatenate(out_parts, axis=1)
    query_grad = jnp.concatenate(query_parts, axis=1)
    grad_pairs = jnp.concatenate(key_parts + value_parts, axis=1)
    window_grads = grad_pairs[:window_rows]
    totals = window_grads[HALO : HALO + tok_rows]
    for direction, edge_rows in ((-1, window_grads[:HALO]), (1, window_grads[HALO + tok_rows :])):
        returned = from_behind(edge_rows.astype(jnp.bfloat16), "tm", direction).astype(
            edge_rows.dtype
        )
        if direction == -1:
            totals = totals.at[tok_rows - HALO :].add(returned)
        else:
            totals = totals.at[:HALO].add(returned)
    far_grads = grad_pairs[window_rows:].reshape(far_slots, TILE, pair_cols)
    for slot, offset in enumerate(offset_list):
        returned = from_behind(far_grads[slot].astype(jnp.bfloat16), "tm", -offset).astype(
            jnp.float32
        )
        reader = jnp.clip(position + offset, 0, block_count - 1)
        chosen = lax.dynamic_slice(far_tiles, (reader, position), (1, 1))[0, 0]
        current = lax.dynamic_slice_in_dim(totals, chosen * TILE, TILE, 0)
        totals = lax.dynamic_update_slice_in_dim(totals, current + returned, chosen * TILE, 0)
    key_grad = totals[:, :head_cols].astype(jnp.bfloat16)
    value_grad = totals[:, head_cols:].astype(jnp.bfloat16)
    return (attended, query_grad, key_grad, value_grad)


def solution(mesh):
    placed = (
        P(("group", "tm"), ("head", "sub")),
        P(("group", "tm"), ("head", "sub")),
        P(("group", "tm"), ("head", "sub")),
        P(("group", "tm"), ("head", "sub")),
        P("tm", None),
        P(),
    )
    return jax.shard_map(
        per_device,
        mesh=mesh,
        in_specs=placed,
        out_specs=(
            P(("group", "tm"), ("head", "sub")),
            P(("group", "tm"), ("head", "sub")),
            P(("group", "tm"), ("head", "sub")),
            P(("group", "tm"), ("head", "sub")),
        ),
        check_vma=False,
    )
```

profile of v0, /device:TPU:0, one launch (start us, length us, event | category | flops | bytes accessed | tf_op | source)
XLA Modules:
  0.0 352.1 jit_solution(18268969052541423862)
XLA Ops:
  3.4 4.2 %collective-permute-start = (bf16[256,3072]{1,0:T(8,128)(2,1)S(1)}, bf16[256,3072]{1,0:T(8,128)(2,1)}, u32[]{:S(2)}, u32[]{:S(2)}) collective-permute-start(bf16[256,3072]{1,0:T(8,128)(2,1)S(1)} %constant_dynamic-update-slice_fusion), channel_id=1, source_target_pairs={{0,2},{2,4},{4,6},{6,8},{8,10},{10,12},{12,14},{14,16},{16,18},{18... | collective-permute-start | bytes 4718600 | tf_op jit(solution)/shard_map/ppermute | solution.py:21
  13.3 2.8 constant_dynamic-slice_fusion
  17.4 7.2 %collective-permute-start.8 = (bf16[128,3072]{1,0:T(8,128)(2,1)}, bf16[128,3072]{1,0:T(8,128)(2,1)}, u32[]{:S(2)}, u32[]{:S(2)}) collective-permute-start(bf16[128,3072]{1,0:T(8,128)(2,1)} %get-tuple-element.69), channel_id=1, source_target_pairs={{0,16},{2,18},{4,20},{6,22},{8,24},{10,26},{12,28},{14,30},{1,17},... | collective-permute-start | bytes 2359304 | tf_op jit(solution)/shard_map/ppermute | solution.py:33
  40.2 12.3 %collective-permute-start.2 = (bf16[128,3072]{1,0:T(8,128)(2,1)}, bf16[128,3072]{1,0:T(8,128)(2,1)S(1)}, u32[]{:S(2)}, u32[]{:S(2)}) collective-permute-start(bf16[128,3072]{1,0:T(8,128)(2,1)} %get-tuple-element.75), channel_id=1, source_target_pairs={{0,2},{2,4},{4,6},{6,8},{8,10},{10,12},{12,14},{14,16},{16,18},{18... | collective-permute-start | bytes 2359304 | tf_op jit(solution)/shard_map/ppermute | solution.py:33
  55.2 4.5 %collective-permute-start.4 = (bf16[128,3072]{1,0:T(8,128)(2,1)S(1)}, bf16[128,3072]{1,0:T(8,128)(2,1)S(1)}, u32[]{:S(2)}, u32[]{:S(2)}) collective-permute-start(bf16[128,3072]{1,0:T(8,128)(2,1)S(1)} %copy-done.40), channel_id=1, source_target_pairs={{0,4},{2,6},{4,8},{6,10},{8,12},{10,14},{12,16},{14,18},{16,20},{1... | collective-permute-start | bytes 2359304 | tf_op jit(solution)/shard_map/ppermute | solution.py:33
  62.8 20.9 %collective-permute-start.6 = (bf16[128,3072]{1,0:T(8,128)(2,1)S(1)}, bf16[128,3072]{1,0:T(8,128)(2,1)S(1)}, u32[]{:S(2)}, u32[]{:S(2)}) collective-permute-start(bf16[128,3072]{1,0:T(8,128)(2,1)S(1)} %copy-done.38), channel_id=1, source_target_pairs={{0,8},{2,10},{4,12},{6,14},{8,16},{10,18},{12,20},{14,22},{16,24},... | collective-permute-start | bytes 2359304 | tf_op jit(solution)/shard_map/ppermute | solution.py:33
  84.9 9.6 %collective-permute-done.4 = bf16[128,3072]{1,0:T(8,128)(2,1)S(1)} collective-permute-done((bf16[128,3072]{1,0:T(8,128)(2,1)S(1)}, bf16[128,3072]{1,0:T(8,128)(2,1)S(1)}, u32[]{:S(2)}, u32[]{:S(2)}) %collective-permute-start.4) | collective-permute-done | bytes 786464 | tf_op jit(solution)/shard_map/ppermute | solution.py:33
  97.5 16.8 %collective-permute-done.7 = bf16[128,3072]{1,0:T(8,128)(2,1)S(1)} collective-permute-done((bf16[128,3072]{1,0:T(8,128)(2,1)S(1)}, bf16[128,3072]{1,0:T(8,128)(2,1)S(1)}, u32[]{:S(2)}, u32[]{:S(2)}) %collective-permute-start.7) | collective-permute-done | bytes 786464 | tf_op jit(solution)/shard_map/ppermute | solution.py:33
  155.4 2.3 copy.58
  157.7 2.8 fusion.88
  161.9 2.1 fusion.90
  165.4 2.1 fusion.92
  168.9 2.1 fusion.94
  172.3 2.1 fusion.96
  175.8 2.1 fusion.98
  179.3 2.1 fusion.100
  182.8 2.1 fusion.102
  207.5 8.0 %convert.16 = bf16[1792,3072]{0,1:T(8,128)(2,1)S(1)} convert(f32[1792,3072]{0,1:T(8,128)} %convolution_dynamic-update-slice_fusion) | non-fusion elementwise | flops 5505024 | bytes 33030144 | tf_op jit(solution)/shard_map/convert.11
  215.5 4.1 %copy-done = bf16[1792,3072]{0,1:T(8,128)(2,1)} copy-done((bf16[1792,3072]{0,1:T(8,128)(2,1)}, bf16[1792,3072]{0,1:T(8,128)(2,1)S(1)}, u32[]{:S(2)}) %copy-start) | copy-done | bytes 11010072
  222.8 5.0 %collective-permute-start.11 = (bf16[256,3072]{0,1:T(8,128)(2,1)}, bf16[256,3072]{0,1:T(8,128)(2,1)S(1)}, u32[]{:S(2)}, u32[]{:S(2)}) collective-permute-start(bf16[256,3072]{0,1:T(8,128)(2,1)} %get-tuple-element.65), channel_id=1, source_target_pairs={{0,2},{2,4},{4,6},{6,8},{8,10},{10,12},{12,14},{14,16},{16,18},{18... | collective-permute-start | bytes 4718600 | tf_op jit(solution)/shard_map/ppermute | solution.py:33
  227.8 2.0 fusion.104
  231.8 2.0 fusion.108
  233.8 2.3 copy.59
  236.1 3.4 fusion.217
  239.5 4.7 %collective-permute-start.19 = (bf16[128,3072]{0,1:T(8,128)(2,1)S(1)}, bf16[128,3072]{0,1:T(8,128)(2,1)S(1)}, u32[]{:S(2)}, u32[]{:S(2)}) collective-permute-start(bf16[128,3072]{0,1:T(8,128)(2,1)S(1)} %get-tuple-element.56), channel_id=1, source_target_pairs={{0,16},{2,18},{4,20},{6,22},{8,24},{10,26},{12,28},{14,30},{1,17},... | collective-permute-start | bytes 2359304 | tf_op jit(solution)/shard_map/ppermute | solution.py:33
  245.5 2.1 collective-permute-start.17
  250.4 2.3 fusion
  252.7 15.0 %collective-permute-done.12 = bf16[128,3072]{0,1:T(8,128)(2,1)S(1)} collective-permute-done((bf16[128,3072]{0,1:T(8,128)(2,1)S(1)}, bf16[128,3072]{0,1:T(8,128)(2,1)S(1)}, u32[]{:S(2)}, u32[]{:S(2)}) %collective-permute-start.12) | collective-permute-done | bytes 786464 | tf_op jit(solution)/shard_map/ppermute | solution.py:33
  269.3 12.6 %collective-permute-start.15 = (bf16[128,3072]{0,1:T(8,128)(2,1)S(1)}, bf16[128,3072]{0,1:T(8,128)(2,1)S(1)}, u32[]{:S(2)}, u32[]{:S(2)}) collective-permute-start(bf16[128,3072]{0,1:T(8,128)(2,1)S(1)} %get-tuple-element.60), channel_id=1, source_target_pairs={{0,4},{2,6},{4,8},{6,10},{8,12},{10,14},{12,16},{14,18},{16,20},{1... | collective-permute-start | bytes 2359304 | tf_op jit(solution)/shard_map/ppermute | solution.py:33
  282.2 7.3 %collective-permute-done.14 = bf16[128,3072]{0,1:T(8,128)(2,1)S(1)} collective-permute-done((bf16[128,3072]{0,1:T(8,128)(2,1)S(1)}, bf16[128,3072]{0,1:T(8,128)(2,1)S(1)}, u32[]{:S(2)}, u32[]{:S(2)}) %collective-permute-start.14) | collective-permute-done | bytes 786464 | tf_op jit(solution)/shard_map/ppermute | solution.py:33
  291.1 28.7 %collective-permute-done.15 = bf16[128,3072]{0,1:T(8,128)(2,1)S(1)} collective-permute-done((bf16[128,3072]{0,1:T(8,128)(2,1)S(1)}, bf16[128,3072]{0,1:T(8,128)(2,1)S(1)}, u32[]{:S(2)}, u32[]{:S(2)}) %collective-permute-start.15) | collective-permute-done | bytes 786464 | tf_op jit(solution)/shard_map/ppermute | solution.py:33
  320.1 27.9 %collective-permute-done.16 = bf16[128,3072]{0,1:T(8,128)(2,1)S(1)} collective-permute-done((bf16[128,3072]{0,1:T(8,128)(2,1)S(1)}, bf16[128,3072]{0,1:T(8,128)(2,1)S(1)}, u32[]{:S(2)}, u32[]{:S(2)}) %collective-permute-start.16) | collective-permute-done | bytes 786464 | tf_op jit(solution)/shard_map/ppermute | solution.py:33
  (284 shorter events, 120.0 us)
Async XLA Ops:
  2.1 52.2 %collective-permute-start.1 = (bf16[256,3072]{1,0:T(8,128)(2,1)S(1)}, bf16[256,3072]{1,0:T(8,128)(2,1)}, u32[]{:S(2)}, u32[]{:S(2)}) collective-permute-start(bf16[256,3072]{1,0:T(8,128)(2,1)S(1)} %constant_dynamic-update-slice_fusion), channel_id=1, source_target_pairs={{2,0},{4,2},{6,4},{8,6},{10,8},{12,10},{14,12},{16,14},{18,16},{20... | collective-permute-start | bytes 4718600 | tf_op jit(solution)/shard_map/ppermute | solution.py:23
  3.4 36.8 %collective-permute-start = (bf16[256,3072]{1,0:T(8,128)(2,1)S(1)}, bf16[256,3072]{1,0:T(8,128)(2,1)}, u32[]{:S(2)}, u32[]{:S(2)}) collective-permute-start(bf16[256,3072]{1,0:T(8,128)(2,1)S(1)} %constant_dynamic-update-slice_fusion), channel_id=1, source_target_pairs={{0,2},{2,4},{4,6},{6,8},{8,10},{10,12},{12,14},{14,16},{16,18},{18... | collective-permute-start | bytes 4718600 | tf_op jit(solution)/shard_map/ppermute | solution.py:21
  13.2 12.6 %copy-start.54 = (s32[2,6]{1,0:T(2,128)S(1)}, s32[2,6]{1,0:T(2,128)}, u32[]{:S(2)}) copy-start(s32[2,6]{1,0:T(2,128)} %param.19) | copy-start | bytes 148
  13.3 12.7 %copy-start.55 = (s32[8]{0:T(128)S(1)}, s32[8]{0:T(128)}, u32[]{:S(2)}) copy-start(s32[8]{0:T(128)} %constant.139) | copy-start | bytes 100
  13.3 13.0 %copy-start.23 = (bf16[256,1536]{1,0:T(8,128)(2,1)S(1)}, bf16[256,1536]{1,0:T(8,128)(2,1)}, u32[]{:S(2)}) copy-start(bf16[256,1536]{1,0:T(8,128)(2,1)} %param.18) | copy-start | bytes 2359300
  16.1 99.6 %collective-permute-start.9 = (bf16[128,3072]{1,0:T(8,128)(2,1)}, bf16[128,3072]{1,0:T(8,128)(2,1)}, u32[]{:S(2)}, u32[]{:S(2)}) collective-permute-start(bf16[128,3072]{1,0:T(8,128)(2,1)} %get-tuple-element.68), channel_id=1, source_target_pairs={{16,0},{18,2},{20,4},{22,6},{24,8},{26,10},{28,12},{30,14},{17,1},... | collective-permute-start | bytes 2359304 | tf_op jit(solution)/shard_map/ppermute | solution.py:33
  17.4 97.0 %collective-permute-start.8 = (bf16[128,3072]{1,0:T(8,128)(2,1)}, bf16[128,3072]{1,0:T(8,128)(2,1)}, u32[]{:S(2)}, u32[]{:S(2)}) collective-permute-start(bf16[128,3072]{1,0:T(8,128)(2,1)} %get-tuple-element.69), channel_id=1, source_target_pairs={{0,16},{2,18},{4,20},{6,22},{8,24},{10,26},{12,28},{14,30},{1,17},... | collective-permute-start | bytes 2359304 | tf_op jit(solution)/shard_map/ppermute | solution.py:33
  24.6 38.2 %collective-permute-start.3 = (bf16[128,3072]{1,0:T(8,128)(2,1)}, bf16[128,3072]{1,0:T(8,128)(2,1)}, u32[]{:S(2)}, u32[]{:S(2)}) collective-permute-start(bf16[128,3072]{1,0:T(8,128)(2,1)} %get-tuple-element.74), channel_id=1, source_target_pairs={{2,0},{4,2},{6,4},{8,6},{10,8},{12,10},{14,12},{16,14},{18,16},{20... | collective-permute-start | bytes 2359304 | tf_op jit(solution)/shard_map/ppermute | solution.py:33
  37.9 16.2 %copy-start.20 = (bf16[256,1536]{1,0:T(8,128)(2,1)S(1)}, bf16[256,1536]{1,0:T(8,128)(2,1)}, u32[]{:S(2)}) copy-start(bf16[256,1536]{1,0:T(8,128)(2,1)} %param.16) | copy-start | bytes 2359300
  40.2 21.0 %collective-permute-start.2 = (bf16[128,3072]{1,0:T(8,128)(2,1)}, bf16[128,3072]{1,0:T(8,128)(2,1)S(1)}, u32[]{:S(2)}, u32[]{:S(2)}) collective-permute-start(bf16[128,3072]{1,0:T(8,128)(2,1)} %get-tuple-element.75), channel_id=1, source_target_pairs={{0,2},{2,4},{4,6},{6,8},{8,10},{10,12},{12,14},{14,16},{16,18},{18... | collective-permute-start | bytes 2359304 | tf_op jit(solution)/shard_map/ppermute | solution.py:33
  55.2 7.6 %copy-start.38 = (bf16[128,3072]{1,0:T(8,128)(2,1)S(1)}, bf16[128,3072]{1,0:T(8,128)(2,1)}, u32[]{:S(2)}) copy-start(bf16[128,3072]{1,0:T(8,128)(2,1)} %get-tuple-element.71) | copy-start | bytes 2359300
  55.2 39.3 %collective-permute-start.4 = (bf16[128,3072]{1,0:T(8,128)(2,1)S(1)}, bf16[128,3072]{1,0:T(8,128)(2,1)S(1)}, u32[]{:S(2)}, u32[]{:S(2)}) collective-permute-start(bf16[128,3072]{1,0:T(8,128)(2,1)S(1)} %copy-done.40), channel_id=1, source_target_pairs={{0,4},{2,6},{4,8},{6,10},{8,12},{10,14},{12,16},{14,18},{16,20},{1... | collective-permute-start | bytes 2359304 | tf_op jit(solution)/shard_map/ppermute | solution.py:33
  61.3 33.3 %copy-start.37 = (bf16[128,3072]{1,0:T(8,128)(2,1)S(1)}, bf16[128,3072]{1,0:T(8,128)(2,1)}, u32[]{:S(2)}) copy-start(bf16[128,3072]{1,0:T(8,128)(2,1)} %get-tuple-element.70) | copy-start | bytes 2359300
  61.3 36.1 %collective-permute-start.5 = (bf16[128,3072]{1,0:T(8,128)(2,1)S(1)}, bf16[128,3072]{1,0:T(8,128)(2,1)S(1)}, u32[]{:S(2)}, u32[]{:S(2)}) collective-permute-start(bf16[128,3072]{1,0:T(8,128)(2,1)S(1)} %copy-done.39), channel_id=1, source_target_pairs={{4,0},{6,2},{8,4},{10,6},{12,8},{14,10},{16,12},{18,14},{20,16},{2... | collective-permute-start | bytes 2359304 | tf_op jit(solution)/shard_map/ppermute | solution.py:33
  62.8 34.6 %collective-permute-start.6 = (bf16[128,3072]{1,0:T(8,128)(2,1)S(1)}, bf16[128,3072]{1,0:T(8,128)(2,1)S(1)}, u32[]{:S(2)}, u32[]{:S(2)}) collective-permute-start(bf16[128,3072]{1,0:T(8,128)(2,1)S(1)} %copy-done.38), channel_id=1, source_target_pairs={{0,8},{2,10},{4,12},{6,14},{8,16},{10,18},{12,20},{14,22},{16,24},... | collective-permute-start | bytes 2359304 | tf_op jit(solution)/shard_map/ppermute | solution.py:33
  94.5 19.8 %collective-permute-start.7 = (bf16[128,3072]{1,0:T(8,128)(2,1)S(1)}, bf16[128,3072]{1,0:T(8,128)(2,1)S(1)}, u32[]{:S(2)}, u32[]{:S(2)}) collective-permute-start(bf16[128,3072]{1,0:T(8,128)(2,1)S(1)} %copy-done.37), channel_id=1, source_target_pairs={{8,0},{10,2},{12,4},{14,6},{16,8},{18,10},{20,12},{22,14},{24,16},... | collective-permute-start | bytes 2359304 | tf_op jit(solution)/shard_map/ppermute | solution.py:33
  116.9 37.0 %copy-start.1 = (bf16[1792,3072]{1,0:T(8,128)(2,1)}, bf16[1792,3072]{1,0:T(8,128)(2,1)S(1)}, u32[]{:S(2)}) copy-start(bf16[1792,3072]{1,0:T(8,128)(2,1)S(1)} %constant_dynamic-update-slice_fusion.2) | copy-start | bytes 33030148
  129.6 18.1 %copy-start.4 = (bf16[256,1792]{0,1:T(8,128)(2,1)}, bf16[256,1792]{0,1:T(8,128)(2,1)S(1)}, u32[]{:S(2)}) copy-start(bf16[256,1792]{0,1:T(8,128)(2,1)S(1)} %fusion.112) | copy-start | bytes 2752516
  130.3 15.6 %copy-start.6 = (bf16[256,1792]{0,1:T(8,128)(2,1)}, bf16[256,1792]{0,1:T(8,128)(2,1)S(1)}, u32[]{:S(2)}) copy-start(bf16[256,1792]{0,1:T(8,128)(2,1)S(1)} %fusion.113) | copy-start | bytes 2752516
  130.9 13.0 %copy-start.8 = (bf16[256,1792]{0,1:T(8,128)(2,1)}, bf16[256,1792]{0,1:T(8,128)(2,1)S(1)}, u32[]{:S(2)}) copy-start(bf16[256,1792]{0,1:T(8,128)(2,1)S(1)} %fusion.114) | copy-start | bytes 2752516
  131.5 10.5 %copy-start.10 = (bf16[256,1792]{0,1:T(8,128)(2,1)}, bf16[256,1792]{0,1:T(8,128)(2,1)S(1)}, u32[]{:S(2)}) copy-start(bf16[256,1792]{0,1:T(8,128)(2,1)S(1)} %fusion.115) | copy-start | bytes 2752516
  132.4 7.8 %copy-start.12 = (bf16[256,1792]{0,1:T(8,128)(2,1)}, bf16[256,1792]{0,1:T(8,128)(2,1)S(1)}, u32[]{:S(2)}) copy-start(bf16[256,1792]{0,1:T(8,128)(2,1)S(1)} %fusion.116) | copy-start | bytes 2752516
  221.6 26.0 %collective-permute-start.10 = (bf16[256,3072]{0,1:T(8,128)(2,1)}, bf16[256,3072]{0,1:T(8,128)(2,1)S(1)}, u32[]{:S(2)}, u32[]{:S(2)}) collective-permute-start(bf16[256,3072]{0,1:T(8,128)(2,1)} %get-tuple-element.64), channel_id=1, source_target_pairs={{2,0},{4,2},{6,4},{8,6},{10,8},{12,10},{14,12},{16,14},{18,16},{20... | collective-permute-start | bytes 4718600 | tf_op jit(solution)/shard_map/ppermute | solution.py:33
  222.8 26.0 %collective-permute-start.11 = (bf16[256,3072]{0,1:T(8,128)(2,1)}, bf16[256,3072]{0,1:T(8,128)(2,1)S(1)}, u32[]{:S(2)}, u32[]{:S(2)}) collective-permute-start(bf16[256,3072]{0,1:T(8,128)(2,1)} %get-tuple-element.65), channel_id=1, source_target_pairs={{0,2},{2,4},{4,6},{6,8},{8,10},{10,12},{12,14},{14,16},{16,18},{18... | collective-permute-start | bytes 4718600 | tf_op jit(solution)/shard_map/ppermute | solution.py:33
  239.5 109.5 %collective-permute-start.19 = (bf16[128,3072]{0,1:T(8,128)(2,1)S(1)}, bf16[128,3072]{0,1:T(8,128)(2,1)S(1)}, u32[]{:S(2)}, u32[]{:S(2)}) collective-permute-start(bf16[128,3072]{0,1:T(8,128)(2,1)S(1)} %get-tuple-element.56), channel_id=1, source_target_pairs={{0,16},{2,18},{4,20},{6,22},{8,24},{10,26},{12,28},{14,30},{1,17},... | collective-permute-start | bytes 2359304 | tf_op jit(solution)/shard_map/ppermute | solution.py:33
  244.2 104.5 %collective-permute-start.18 = (bf16[128,3072]{0,1:T(8,128)(2,1)S(1)}, bf16[128,3072]{0,1:T(8,128)(2,1)S(1)}, u32[]{:S(2)}, u32[]{:S(2)}) collective-permute-start(bf16[128,3072]{0,1:T(8,128)(2,1)S(1)} %get-tuple-element.57), channel_id=1, source_target_pairs={{16,0},{18,2},{20,4},{22,6},{24,8},{26,10},{28,12},{30,14},{17,1},... | collective-permute-start | bytes 2359304 | tf_op jit(solution)/shard_map/ppermute | solution.py:33
  245.5 102.9 %collective-permute-start.17 = (bf16[128,3072]{0,1:T(8,128)(2,1)S(1)}, bf16[128,3072]{0,1:T(8,128)(2,1)S(1)}, u32[]{:S(2)}, u32[]{:S(2)}) collective-permute-start(bf16[128,3072]{0,1:T(8,128)(2,1)S(1)} %get-tuple-element.58), channel_id=1, source_target_pairs={{0,8},{2,10},{4,12},{6,14},{8,16},{10,18},{12,20},{14,22},{16,24},... | collective-permute-start | bytes 2359304 | tf_op jit(solution)/shard_map/ppermute | solution.py:33
  247.5 21.7 %collective-permute-start.13 = (bf16[128,3072]{0,1:T(8,128)(2,1)S(1)}, bf16[128,3072]{0,1:T(8,128)(2,1)S(1)}, u32[]{:S(2)}, u32[]{:S(2)}) collective-permute-start(bf16[128,3072]{0,1:T(8,128)(2,1)S(1)} %get-tuple-element.62), channel_id=1, source_target_pairs={{0,2},{2,4},{4,6},{6,8},{8,10},{10,12},{12,14},{14,16},{16,18},{18... | collective-permute-start | bytes 2359304 | tf_op jit(solution)/shard_map/ppermute | solution.py:33
  248.9 18.8 %collective-permute-start.12 = (bf16[128,3072]{0,1:T(8,128)(2,1)S(1)}, bf16[128,3072]{0,1:T(8,128)(2,1)S(1)}, u32[]{:S(2)}, u32[]{:S(2)}) collective-permute-start(bf16[128,3072]{0,1:T(8,128)(2,1)S(1)} %get-tuple-element.63), channel_id=1, source_target_pairs={{2,0},{4,2},{6,4},{8,6},{10,8},{12,10},{14,12},{16,14},{18,16},{20... | collective-permute-start | bytes 2359304 | tf_op jit(solution)/shard_map/ppermute | solution.py:33
  267.7 21.9 %collective-permute-start.14 = (bf16[128,3072]{0,1:T(8,128)(2,1)S(1)}, bf16[128,3072]{0,1:T(8,128)(2,1)S(1)}, u32[]{:S(2)}, u32[]{:S(2)}) collective-permute-start(bf16[128,3072]{0,1:T(8,128)(2,1)S(1)} %get-tuple-element.61), channel_id=1, source_target_pairs={{4,0},{6,2},{8,4},{10,6},{12,8},{14,10},{16,12},{18,14},{20,16},{2... | collective-permute-start | bytes 2359304 | tf_op jit(solution)/shard_map/ppermute | solution.py:33
  269.3 50.5 %collective-permute-start.15 = (bf16[128,3072]{0,1:T(8,128)(2,1)S(1)}, bf16[128,3072]{0,1:T(8,128)(2,1)S(1)}, u32[]{:S(2)}, u32[]{:S(2)}) collective-permute-start(bf16[128,3072]{0,1:T(8,128)(2,1)S(1)} %get-tuple-element.60), channel_id=1, source_target_pairs={{0,4},{2,6},{4,8},{6,10},{8,12},{10,14},{12,16},{14,18},{16,20},{1... | collective-permute-start | bytes 2359304 | tf_op jit(solution)/shard_map/ppermute | solution.py:33
  289.5 58.5 %collective-permute-start.16 = (bf16[128,3072]{0,1:T(8,128)(2,1)S(1)}, bf16[128,3072]{0,1:T(8,128)(2,1)S(1)}, u32[]{:S(2)}, u32[]{:S(2)}) collective-permute-start(bf16[128,3072]{0,1:T(8,128)(2,1)S(1)} %get-tuple-element.59), channel_id=1, source_target_pairs={{8,0},{10,2},{12,4},{14,6},{16,8},{18,10},{20,12},{22,14},{24,16},... | collective-permute-start | bytes 2359304 | tf_op jit(solution)/shard_map/ppermute | solution.py:33
  (44 other events, 121.9 us)
where the time goes:
time: 357 us; the launch traced here: 352 us
  waiting for transfers between devices  107 us (30%)
  starting transfers between devices  88.1 us (25%)
  matrix products  84.9 us (24%)
  local copies, waits for them, and re-layouts  44.3 us (12%)
  other arithmetic  21.2 us (6%)
  between operations  6.93 us (2%)
    ppermute x18, waiting for transfers between devices, from_behind(): lax.ppermute(value, axis, [(source, source + steps) for source in range(l...  107 us
    ppermute x18, starting transfers between devices, from_behind(): lax.ppermute(value, axis, [(source, source + steps) for source in range(l...  82.7 us
    unnamed x144, local copies, waits for them, and re-layouts  34 us
    dot_general x12, matrix products, per_device(): jnp.dot(dscores, key_head, preferred_element_type=jnp.float32) * score_scale  24.3 us
    dot_general x12, matrix products, per_device(): jnp.einsum('qk,qd->kd', dscores, query_head, preferred_element_type=jnp.f...  16.9 us
    dot_general x12, matrix products, per_device(): jnp.einsum('qk,qd->kd', weights_b, grad_head, preferred_element_type=jnp....  16.8 us
    dot_general x12, matrix products, per_device(): jnp.einsum('qd,kd->qk', grad_head, value_head, preferred_element_type=jnp...  16.8 us
    another operation x2, other arithmetic  8.18 us
  transfers between devices with their start and end apart: 20, of which 7 were waited for; matrix products, arithmetic and copies ran while one was open for 11% of the time, Pallas kernels for 0%

commit v1 on v0

v1 whole, which is shorter than its diff:
```python
import functools
import math

import jax
import jax.numpy as jnp
from jax import lax
from jax.experimental import pallas as pl
from jax.experimental.pallas import tpu as pltpu
from jax.sharding import PartitionSpec as P

D_HEAD = 128
TILE = 128
MESH = pl.DeviceIdType.MESH


def far_strides(count):
    strides = []
    stride = 2
    while stride < count:
        strides += [stride, -stride]
        stride *= 2
    return strides


def kernel(
    n, chunk, q_ref, k_ref, v_ref, g_ref, band_ref, far_ref, o_ref, dq_ref, dk_ref, dv_ref,
    kv, picked, bias, marks, own, gsend, grecv, send_sem, recv_sem, gsend_sem, grecv_sem,
):
    tok, cols_all = q_ref.shape
    heads = cols_all // D_HEAD
    chunks = heads // chunk
    width = 2 * D_HEAD * chunk
    tiles = tok // TILE
    rows = kv.shape[0]
    pos = lax.axis_index("tm")
    scale = 1.0 / math.sqrt(D_HEAD)
    far = far_strides(n)
    slots = [(1, tok, tok), (-1, 2 * tok, tok)]
    slots += [(d, 3 * tok + j * TILE, TILE) for j, d in enumerate(far)]
    order = list(range(len(slots)))[::-1]

    def within(index):
        return (index >= 0) & (index < n)

    barrier = pltpu.get_barrier_semaphore()
    partners = jnp.int32(0)
    for d, _, _ in slots:
        partners = partners + within(pos + d).astype(jnp.int32)

        @pl.when(within(pos + d))
        def _():
            pl.semaphore_signal(barrier, inc=1, device_id={"tm": pos + d}, device_id_type=MESH)

    pl.semaphore_wait(barrier, partners)

    def span(c):
        return pl.ds(pl.multiple_of(c * width, 2 * D_HEAD), width)

    def key_send(s, c):
        d, row, count = slots[s]
        if s < 2:
            src = kv.at[pl.ds(0, tok), span(c)]
        else:
            src = picked.at[pl.ds((s - 2) * TILE, TILE), span(c)]
        return pltpu.make_async_remote_copy(
            src_ref=src, dst_ref=kv.at[pl.ds(row, count), span(c)],
            send_sem=send_sem.at[s, c], recv_sem=recv_sem.at[s, c],
            device_id={"tm": pos + d}, device_id_type=MESH,
        )

    def key_recv(s, c):
        d, row, count = slots[s]
        ref = kv.at[pl.ds(row, count), span(c)]
        return pltpu.make_async_remote_copy(
            src_ref=ref, dst_ref=ref, send_sem=send_sem.at[s, c], recv_sem=recv_sem.at[s, c],
            device_id={"tm": pos - d}, device_id_type=MESH,
        )

    def grad_send(s, c):
        d, row, count = slots[s]
        at = pl.ds(row - tok, count)
        return pltpu.make_async_remote_copy(
            src_ref=gsend.at[at, span(c)], dst_ref=grecv.at[at, span(c)],
            send_sem=gsend_sem.at[s, c], recv_sem=grecv_sem.at[s, c],
            device_id={"tm": pos - d}, device_id_type=MESH,
        )

    def grad_recv(s, c):
        d, row, count = slots[s]
        ref = grecv.at[pl.ds(row - tok, count), span(c)]
        return pltpu.make_async_remote_copy(
            src_ref=ref, dst_ref=ref, send_sem=gsend_sem.at[s, c], recv_sem=grecv_sem.at[s, c],
            device_id={"tm": pos + d}, device_id_type=MESH,
        )

    def far_entry(reader, source):
        line = far_ref[pl.ds(jnp.clip(reader, 0, n - 1), 1), :].astype(jnp.float32)
        here = lax.broadcasted_iota(jnp.int32, line.shape, 1) == jnp.clip(source, 0, n - 1)
        return jnp.sum(jnp.where(here, line, 0.0), axis=1, keepdims=True)

    for j, d in enumerate(far):
        marks[pl.ds(j, 1), :] = jnp.broadcast_to(far_entry(pos + d, pos), (1, D_HEAD))

    def pick(ref, j, cols):
        out = ref[pl.ds(0, TILE), cols].astype(jnp.float32)
        for t in range(1, tiles):
            here = jnp.broadcast_to(marks[pl.ds(j, 1), :], (TILE, D_HEAD)) == float(t)
            out = jnp.where(here, ref[pl.ds(t * TILE, TILE), cols].astype(jnp.float32), out)
        return out.astype(ref.dtype)

    def push(c, carry):
        for i in range(chunk):
            h = c * chunk + i
            narrow = pl.ds(pl.multiple_of(h * D_HEAD, D_HEAD), D_HEAD)
            k_cols = pl.ds(pl.multiple_of(h * 2 * D_HEAD, D_HEAD), D_HEAD)
            v_cols = pl.ds(pl.multiple_of(h * 2 * D_HEAD + D_HEAD, D_HEAD), D_HEAD)
            for j, d in enumerate(far):
                picked[pl.ds(j * TILE, TILE), k_cols] = pick(k_ref, j, narrow)
                picked[pl.ds(j * TILE, TILE), v_cols] = pick(v_ref, j, narrow)
            kv[pl.ds(0, tok), k_cols] = k_ref[:, narrow]
            kv[pl.ds(0, tok), v_cols] = v_ref[:, narrow]
        for s in order:
            @pl.when(within(pos + slots[s][0]))
            def _():
                key_send(s, c).start()
        return carry

    lax.fori_loop(0, chunks, push, 0)

    for d, row, count in slots:
        @pl.when(jnp.logical_not(within(pos - d)))
        def _():
            kv[pl.ds(row, count), :] = jnp.zeros((count, kv.shape[1]), kv.dtype)

    lane = lax.broadcasted_iota(jnp.int32, (1, tok), 1) // TILE

    for t in range(rows // TILE):
        if t < 3 * tiles:
            block = t // tiles
            shift = (0, -1, 1)[block]
            at = t % tiles
            window = tiles * (1 + shift) + at
            times = jnp.zeros((1, tok), jnp.float32)
            for a in range(tiles):
                on = (band_ref[a : a + 1, window : window + 1] != 0).astype(jnp.float32)
                times = jnp.where(lane == a, jnp.broadcast_to(on, (1, tok)), times)
            if block:
                extra = (far_entry(pos, pos + shift) == float(at)).astype(jnp.float32)
                times = times + jnp.broadcast_to(extra, (1, tok))
        else:
            shift = -far[t - 3 * tiles]
            times = jnp.ones((1, tok), jnp.float32)
        times = times * within(pos + shift).astype(jnp.float32)
        bias[pl.ds(t, 1), :] = jnp.where(times == 0.0, -1e30, times - 1.0)

    lines = rows // TILE

    def head(h, carry):
        narrow = pl.ds(pl.multiple_of(h * D_HEAD, D_HEAD), D_HEAD)
        k_cols = pl.ds(pl.multiple_of(h * 2 * D_HEAD, D_HEAD), D_HEAD)
        v_cols = pl.ds(pl.multiple_of(h * 2 * D_HEAD + D_HEAD, D_HEAD), D_HEAD)
        q, g = q_ref[:, narrow], g_ref[:, narrow]
        k, v = kv[:, k_cols], kv[:, v_cols]
        last = (((1,), (1,)), ((), ()))
        first = (((0,), (0,)), ((), ()))
        f32 = jnp.float32
        scores = lax.dot_general(k, q, last, preferred_element_type=f32)
        scores = scores.reshape(lines, TILE, tok) * (scale * math.log2(math.e))
        scores = (scores + bias[0:lines, :][:, None, :]).reshape(rows, tok)
        raised = jnp.exp2(scores - jnp.max(scores, axis=0, keepdims=True))
        weights = raised * (1.0 / jnp.sum(raised, axis=0, keepdims=True))
        weights_b = weights.astype(jnp.bfloat16)
        out = lax.dot_general(v, weights_b, first, preferred_element_type=f32)
        out_b = out.T.astype(jnp.bfloat16)
        o_ref[:, narrow] = out_b
        out_t = out.astype(jnp.bfloat16).astype(f32)
        delta = jnp.sum(g.astype(f32).T * out_t, axis=0, keepdims=True)
        dweights = lax.dot_general(v, g, last, preferred_element_type=f32)
        dscores = (weights * (dweights - delta)).astype(jnp.bfloat16)
        dq = lax.dot_general(k, dscores, first, preferred_element_type=f32) * scale
        dq_ref[:, narrow] = dq.T.astype(jnp.bfloat16)
        dk = jnp.dot(dscores, q, preferred_element_type=f32) * scale
        dv = jnp.dot(weights_b, g, preferred_element_type=f32)
        own[:, k_cols] = dk[:tok]
        own[:, v_cols] = dv[:tok]
        gsend[:, k_cols] = dk[tok:].astype(jnp.bfloat16)
        gsend[:, v_cols] = dv[tok:].astype(jnp.bfloat16)
        return carry

    def work(c, carry):
        for s in order:
            @pl.when(within(pos - slots[s][0]))
            def _():
                key_recv(s, c).wait_recv()

        lax.fori_loop(c * chunk, (c + 1) * chunk, head, 0)
        for s in order:
            @pl.when(within(pos - slots[s][0]))
            def _():
                grad_send(s, c).start()
        return carry

    lax.fori_loop(0, chunks, work, 0)

    for d, row, count in slots:
        @pl.when(jnp.logical_not(within(pos + d)))
        def _():
            grecv[pl.ds(row - tok, count), :] = jnp.zeros((count, grecv.shape[1]), grecv.dtype)

    def gather(c, carry):
        for s in order:
            @pl.when(within(pos + slots[s][0]))
            def _():
                grad_recv(s, c).wait_recv()

        for i in range(chunk):
            h = c * chunk + i
            narrow = pl.ds(pl.multiple_of(h * D_HEAD, D_HEAD), D_HEAD)
            for part, ref in ((0, dk_ref), (1, dv_ref)):
                cols = pl.ds(pl.multiple_of(h * 2 * D_HEAD + part * D_HEAD, D_HEAD), D_HEAD)
                for t in range(tiles):
                    at = pl.ds(t * TILE, TILE)
                    total = own[at, cols]
                    for _, row, _ in slots[:2]:
                        total = total + grecv[pl.ds(row - tok + t * TILE, TILE), cols].astype(
                            jnp.float32
                        )
                    for j, (_, row, _) in enumerate(slots[2:]):
                        here = (marks[pl.ds(j, 1), :] == float(t)).astype(jnp.float32)
                        total = total + here * grecv[pl.ds(row - tok, TILE), cols].astype(
                            jnp.float32
                        )
                    ref[at, narrow] = total.astype(jnp.bfloat16)
        return carry

    lax.fori_loop(0, chunks, gather, 0)

    def drain(c, carry):
        for s in order:
            @pl.when(within(pos + slots[s][0]))
            def _():
                key_send(s, c).wait_send()

            @pl.when(within(pos - slots[s][0]))
            def _():
                grad_send(s, c).wait_send()
        return carry

    lax.fori_loop(0, chunks, drain, 0)


def per_device(queries, keys_in, values_in, out_grad, band_mask, far_tiles):
    tok, cols = queries.shape
    heads = cols // D_HEAD
    n = lax.axis_size("tm")
    chunk = 2 if heads % 2 == 0 else 1
    chunks = heads // chunk
    slots = 2 + len(far_strides(n))
    rows = 3 * tok + (slots - 2) * TILE
    lines = -(-rows // TILE // 8) * 8
    flops = 2 * 6 * tok * rows * cols
    bf16 = jnp.bfloat16
    vmem = pl.BlockSpec(memory_space=pltpu.VMEM)
    out = jax.ShapeDtypeStruct((tok, cols), bf16)
    sems = pltpu.SemaphoreType.DMA((slots, chunks))
    return pl.pallas_call(
        functools.partial(kernel, n, chunk),
        out_shape=(out,) * 4,
        in_specs=[vmem] * 6,
        out_specs=(vmem,) * 4,
        scratch_shapes=[
            pltpu.VMEM((rows, 2 * cols), bf16),
            pltpu.VMEM((rows - 3 * tok, 2 * cols), bf16),
            pltpu.VMEM((lines, tok), jnp.float32),
            pltpu.VMEM((max(8, slots), D_HEAD), jnp.float32),
            pltpu.VMEM((tok, 2 * cols), jnp.float32),
            pltpu.VMEM((rows - tok, 2 * cols), bf16),
            pltpu.VMEM((rows - tok, 2 * cols), bf16),
            sems, sems, sems, sems,
        ],
        compiler_params=pltpu.CompilerParams(
            collective_id=0, has_side_effects=True, vmem_limit_bytes=60 * 1024 * 1024
        ),
        cost_estimate=pl.CostEstimate(
            flops=flops, bytes_accessed=16 * tok * cols, transcendentals=tok * rows * heads
        ),
    )(queries, keys_in, values_in, out_grad, band_mask, far_tiles)


def solution(mesh):
    cells = P(("group", "tm"), ("head", "sub"))
    return jax.shard_map(
        per_device,
        mesh=mesh,
        in_specs=(cells,) * 4 + (P("tm", None), P()),
        out_specs=(cells,) * 4,
        check_vma=False,
    )
```

time: 357 us -> 186 us (0.52)
  the two profiles are of different devices: /device:TPU:0 before, /device:TPU:18 now
where the time goes in v1:
time: 186 us
  Pallas kernels  180 us (97%)
  local copies, waits for them, and re-layouts  5.85 us (3%)
    pallas_call x1, Pallas kernels, per_device(): pl.pallas_call(functools.partial(kernel, n, chunk), out_shape=(out,) * 4,...  180 us
    unnamed x10, local copies, waits for them, and re-layouts  5.85 us

profile of v1, /device:TPU:18, one launch (start us, length us, event | category | flops | bytes accessed | tf_op | source)
XLA Modules:
  0.0 186.1 jit_solution(7660071011499818900)
XLA Ops:
  0.6 179.6 %shard_map.93 = (bf16[256,1536]{1,0:T(8,128)(2,1)}, bf16[256,1536]{1,0:T(8,128)(2,1)}, bf16[256,1536]{1,0:T(8,128)(2,1)}, bf16[256,1536]{1,0:T(8,128)(2,1)}) custom-call(bf16[256,1536]{1,0:T(8,128)(2,1)} %q_ref.1, bf16[256,1536]{1,0:T(8,128)(2,1)} %k_ref.1, bf16[256,1536]{1,0:T(8,128)(2,1)} %v_ref.1, bf16[256,1536]{1,0:T(8,128)(2,1)} %g_ref.1, ...), custom_call_target="tpu_custom_call" | custom-call | flops 7247757312 | bytes 6291456 | tf_op jit(solution)/shard_map/pallas_call | solution.py:266
  180.2 0.0 copy-start.2
  180.2 2.1 %copy.14 = bf16[256,1536]{1,0:T(8,128)(2,1)} copy(bf16[256,1536]{1,0:T(8,128)(2,1)} %get-tuple-element.8) | data formatting | bytes 1572864
  182.4 0.0 copy-done.2
  182.4 0.0 copy-start.1
  182.4 0.9 copy.15
  183.2 0.5 copy-done.1
  183.8 0.0 copy-start
  183.8 0.9 copy.16
  184.7 0.5 copy-done
  185.2 0.9 copy.17
Async XLA Ops:
  180.2 2.1 %copy-start.2 = (bf16[256,1536]{1,0:T(8,128)(2,1)S(1)}, bf16[256,1536]{1,0:T(8,128)(2,1)}, u32[]{:S(2)}) copy-start(bf16[256,1536]{1,0:T(8,128)(2,1)} %get-tuple-element.9) | copy-start | bytes 2359300
  182.4 1.4 copy-start.1
  183.8 1.4 copy-start

commit v2 on v1

--- a/solution.py
+++ b/solution.py
@@ -10,6 +10,7 @@
 
 D_HEAD = 128
 TILE = 128
+LEAD = 3
 MESH = pl.DeviceIdType.MESH
 
 
@@ -24,11 +25,13 @@
 
 def kernel(
     n, chunk, q_ref, k_ref, v_ref, g_ref, band_ref, far_ref, o_ref, dq_ref, dk_ref, dv_ref,
-    kv, picked, bias, marks, own, gsend, grecv, send_sem, recv_sem, gsend_sem, grecv_sem,
+    kv, picked, bias, marks, own, gsend, grecv, passed, cut, folded, joined,
+    send_sem, recv_sem, gsend_sem, grecv_sem, xsend_sem, xrecv_sem,
 ):
     tok, cols_all = q_ref.shape
     heads = cols_all // D_HEAD
     chunks = heads // chunk
+    lead = min(LEAD, chunks)
     width = 2 * D_HEAD * chunk
     tiles = tok // TILE
     rows = kv.shape[0]
@@ -42,9 +45,46 @@
     def within(index):
         return (index >= 0) & (index < n)
 
+    odd = lax.rem(pos, 2)
+    side = 1 - 2 * odd
+    mate = pos + side
+    cuts = within(pos - side)
+    quarter = lax.rem(pos, 4)
+    third, zeroth = quarter == 3, quarter == 0
+    ahead = jnp.where(third, 1, -1)
+    passer = third | zeroth
+    passes = passer & within(pos - 4 * ahead)
+    starts = passer & within(pos + 4 * ahead)
+    pass_slot = jnp.where(third, 0, 1)
+    cut_mark, keep_mark = len(far), len(far) + 1
+    direct = [
+        jnp.logical_not(third), jnp.logical_not(zeroth), odd == 0, odd == 1,
+        jnp.logical_not(third), jnp.logical_not(zeroth),
+    ]
+    direct += [jnp.bool_(True)] * (len(slots) - 6)
+
+    def key_out(s):
+        return within(pos + slots[s][0]) & direct[s]
+
+    def key_in(s):
+        live = within(pos - slots[s][0])
+        if s < 2:
+            return live & (odd == 1 - s)
+        return live & direct[s] if s in (4, 5) else live
+
+    def grad_out(s):
+        live = within(pos - slots[s][0])
+        if s < 2:
+            return live & (odd == 1 - s)
+        return live & direct[s] if s in (4, 5) else live
+
+    def grad_in(s):
+        live = within(pos + slots[s][0])
+        return live if s < 2 else live & direct[s]
+
     barrier = pltpu.get_barrier_semaphore()
     partners = jnp.int32(0)
-    for d, _, _ in slots:
+    for d in [d for d, _, _ in slots] + [3, -3]:
         partners = partners + within(pos + d).astype(jnp.int32)
 
         @pl.when(within(pos + d))
@@ -76,14 +116,100 @@
             device_id={"tm": pos - d}, device_id_type=MESH,
         )
 
+    def remote(src, dst, sent, arrived, to):
+        return pltpu.make_async_remote_copy(
+            src_ref=src, dst_ref=dst, send_sem=sent, recv_sem=arrived,
+            device_id={"tm": to}, device_id_type=MESH,
+        )
+
+    def start_send(c):
+        return remote(
+            kv.at[pl.ds(0, tok), span(c)], passed.at[:, span(c)],
+            xsend_sem.at[3, c], xrecv_sem.at[0, c], pos + 4 * ahead,
+        )
+
+    def pass_recv(c):
+        ref = passed.at[:, span(c)]
+        return remote(ref, ref, xsend_sem.at[3, c], xrecv_sem.at[0, c], pos - 4 * ahead)
+
+    def pass_send(c):
+        row = pl.multiple_of(tok * (1 + pass_slot), tok)
+        return remote(
+            passed.at[:, span(c)], kv.at[pl.ds(row, tok), span(c)],
+            xsend_sem.at[0, c], recv_sem.at[pass_slot, c], pos - 3 * ahead,
+        )
+
+    def whole_recv(c):
+        ref = kv.at[pl.ds(pl.multiple_of(tok * (1 + odd), tok), tok), span(c)]
+        return remote(ref, ref, send_sem.at[odd, c], recv_sem.at[odd, c], pos - side)
+
+    def cut_send(c):
+        row = pl.multiple_of(3 * tok + odd * TILE, TILE)
+        return remote(
+            cut.at[:, span(c)], kv.at[pl.ds(row, TILE), span(c)],
+            xsend_sem.at[1, c], recv_sem.at[2 + odd, c], mate,
+        )
+
+    def fold_recv(c):
+        ref = folded.at[:, span(c)]
+        return remote(ref, ref, xsend_sem.at[1, c], xrecv_sem.at[1, c], mate)
+
+    def whole_rows():
+        return pl.ds(pl.multiple_of(odd * tok, tok), tok)
+
+    def fold_send(c):
+        return remote(
+            gsend.at[whole_rows(), span(c)], grecv.at[whole_rows(), span(c)],
+            gsend_sem.at[odd, c], grecv_sem.at[odd, c], pos - side,
+        )
+
+    def fold_send_pass(c):
+        return remote(
+            gsend.at[whole_rows(), span(c)], joined.at[:, span(c)],
+            gsend_sem.at[odd, c], xrecv_sem.at[2, c], pos + 3 * side,
+        )
+
+    def join_recv(c):
+        ref = joined.at[:, span(c)]
+        return remote(ref, ref, xsend_sem.at[2, c], xrecv_sem.at[2, c], pos - 3 * ahead)
+
+    def join_send(c):
+        row = pl.multiple_of(tok * pass_slot, tok)
+        return remote(
+            joined.at[:, span(c)], grecv.at[pl.ds(row, tok), span(c)],
+            xsend_sem.at[2, c], grecv_sem.at[pass_slot, c], pos - 4 * ahead,
+        )
+
     def grad_send(s, c):
         d, row, count = slots[s]
-        at = pl.ds(row - tok, count)
-        return pltpu.make_async_remote_copy(
-            src_ref=gsend.at[at, span(c)], dst_ref=grecv.at[at, span(c)],
-            send_sem=gsend_sem.at[s, c], recv_sem=grecv_sem.at[s, c],
-            device_id={"tm": pos - d}, device_id_type=MESH,
-        )
+        src = gsend.at[pl.ds(row - tok, count), span(c)]
+        return remote(
+            src, grecv.at[pl.ds(row - tok, count), span(c)],
+            gsend_sem.at[s, c], grecv_sem.at[s, c], pos - d,
+        )
+
+    def mate_send(s, c):
+        d, row, count = slots[s]
+        src = gsend.at[pl.ds(row - tok, count), span(c)]
+        return remote(
+            src, folded.at[:, span(c)], gsend_sem.at[s, c], xrecv_sem.at[1, c], mate
+        )
+
+    def send_grad(s, c, action):
+        if s in (2, 3):
+            to_mate = odd == 3 - s
+
+            @pl.when(grad_out(s) & to_mate)
+            def _():
+                action(mate_send(s, c))
+
+            @pl.when(grad_out(s) & jnp.logical_not(to_mate))
+            def _():
+                action(grad_send(s, c))
+        else:
+            @pl.when(grad_out(s))
+            def _():
+                action(grad_send(s, c))
 
     def grad_recv(s, c):
         d, row, count = slots[s]
@@ -101,12 +227,32 @@
     for j, d in enumerate(far):
         marks[pl.ds(j, 1), :] = jnp.broadcast_to(far_entry(pos + d, pos), (1, D_HEAD))
 
-    def pick(ref, j, cols):
-        out = ref[pl.ds(0, TILE), cols].astype(jnp.float32)
-        for t in range(1, tiles):
+    marks[pl.ds(cut_mark, 1), :] = jnp.broadcast_to(
+        far_entry(mate, pos - side), (1, D_HEAD)
+    )
+    marks[pl.ds(keep_mark, 1), :] = jnp.broadcast_to(
+        far_entry(pos, pos - 4 * ahead), (1, D_HEAD)
+    )
+
+    def pick(ref, j, cols, base=0):
+        out = None
+        for t in range(tiles):
+            row = base + t * TILE
+            if not isinstance(row, int):
+                row = pl.multiple_of(row, TILE)
+            part = ref[pl.ds(row, TILE), cols].astype(jnp.float32)
             here = jnp.broadcast_to(marks[pl.ds(j, 1), :], (TILE, D_HEAD)) == float(t)
-            out = jnp.where(here, ref[pl.ds(t * TILE, TILE), cols].astype(jnp.float32), out)
+            out = part if out is None else jnp.where(here, part, out)
         return out.astype(ref.dtype)
+
+    def add_tile(ref, base, extra, j, cols):
+        for t in range(tiles):
+            row = base + t * TILE
+            if not isinstance(row, int):
+                row = pl.multiple_of(row, TILE)
+            here = (marks[pl.ds(j, 1), :] == float(t)).astype(jnp.float32)
+            total = ref[pl.ds(row, TILE), cols].astype(jnp.float32) + here * extra
+            ref[pl.ds(row, TILE), cols] = total.astype(ref.dtype)
 
     def push(c, carry):
         for i in range(chunk):
@@ -119,13 +265,17 @@
                 picked[pl.ds(j * TILE, TILE), v_cols] = pick(v_ref, j, narrow)
             kv[pl.ds(0, tok), k_cols] = k_ref[:, narrow]
             kv[pl.ds(0, tok), v_cols] = v_ref[:, narrow]
+        @pl.when(starts)
+        def _():
+            start_send(c).start()
+
         for s in order:
-            @pl.when(within(pos + slots[s][0]))
+            @pl.when(key_out(s))
             def _():
                 key_send(s, c).start()
         return carry
 
-    lax.fori_loop(0, chunks, push, 0)
+    lax.fori_loop(0, lead, push, 0)
 
     for d, row, count in slots:
         @pl.when(jnp.logical_not(within(pos - d)))
@@ -187,29 +337,87 @@
         gsend[:, v_cols] = dv[tok:].astype(jnp.bfloat16)
         return carry
 
+    def piece(c, i):
+        return pl.ds(pl.multiple_of(c * width + i * D_HEAD, D_HEAD), D_HEAD)
+
+    def fold(c):
+        @pl.when(cuts)
+        def _():
+            fold_recv(c).wait_recv()
+            for i in range(2 * chunk):
+                extra = folded[:, piece(c, i)].astype(jnp.float32)
+                add_tile(gsend, odd * tok, extra, cut_mark, piece(c, i))
+
+        @pl.when(cuts & passer)
+        def _():
+            fold_send_pass(c).start()
+
+        @pl.when(cuts & jnp.logical_not(passer))
+        def _():
+            fold_send(c).start()
+
+    def join(c):
+        @pl.when(passes)
+        def _():
+            join_recv(c).wait_recv()
+            row = pl.multiple_of(2 * tok + (2 + pass_slot) * TILE, TILE)
+            for i in range(2 * chunk):
+                extra = gsend[pl.ds(row, TILE), piece(c, i)].astype(jnp.float32)
+                add_tile(joined, 0, extra, keep_mark, piece(c, i))
+            join_send(c).start()
+
     def work(c, carry):
+        @pl.when(c + lead < chunks)
+        def _():
+            push(c + lead, 0)
+
+        @pl.when(passes)
+        def _():
+            pass_recv(c).wait_recv()
+            pass_send(c).start()
+            row = pl.multiple_of(3 * tok + (2 + pass_slot) * TILE, TILE)
+            for i in range(2 * chunk):
+                kv[pl.ds(row, TILE), piece(c, i)] = pick(passed, keep_mark, piece(c, i))
+
+        @pl.when(cuts)
+        def _():
+            whole_recv(c).wait_recv()
+            for i in range(2 * chunk):
+                cut[:, piece(c, i)] = pick(kv, cut_mark, piece(c, i), tok * (1 + odd))
+            cut_send(c).start()
+
         for s in order:
-            @pl.when(within(pos - slots[s][0]))
+            @pl.when(key_in(s))
             def _():
                 key_recv(s, c).wait_recv()
 
         lax.fori_loop(c * chunk, (c + 1) * chunk, head, 0)
         for s in order:
-            @pl.when(within(pos - slots[s][0]))
-            def _():
-                grad_send(s, c).start()
+            send_grad(s, c, lambda copy: copy.start())
+
+        @pl.when(c >= 1)
+        def _():
+            fold(c - 1)
+
+        @pl.when(c >= 2)
+        def _():
+            join(c - 2)
         return carry
 
     lax.fori_loop(0, chunks, work, 0)
+    fold(chunks - 1)
+    if chunks > 1:
+        join(chunks - 2)
+    join(chunks - 1)
 
     for d, row, count in slots:
-        @pl.when(jnp.logical_not(within(pos + d)))
+        @pl.when(jnp.logical_not(grad_in(slots.index((d, row, count)))))
         def _():
             grecv[pl.ds(row - tok, count), :] = jnp.zeros((count, grecv.shape[1]), grecv.dtype)
 
     def gather(c, carry):
         for s in order:
-            @pl.when(within(pos + slots[s][0]))
+            @pl.when(grad_in(s))
             def _():
                 grad_recv(s, c).wait_recv()
 
@@ -237,13 +445,32 @@
 
     def drain(c, carry):
         for s in order:
-            @pl.when(within(pos + slots[s][0]))
+            @pl.when(key_out(s))
             def _():
                 key_send(s, c).wait_send()
 
-            @pl.when(within(pos - slots[s][0]))
-            def _():
-                grad_send(s, c).wait_send()
+            send_grad(s, c, lambda copy: copy.wait_send())
+
+        @pl.when(starts)
+        def _():
+            start_send(c).wait_send()
+
+        @pl.when(passes)
+        def _():
+            pass_send(c).wait_send()
+            join_send(c).wait_send()
+
+        @pl.when(cuts)
+        def _():
+            cut_send(c).wait_send()
+
+        @pl.when(cuts & passer)
+        def _():
+            fold_send_pass(c).wait_send()
+
+        @pl.when(cuts & jnp.logical_not(passer))
+        def _():
+            fold_send(c).wait_send()
         return carry
 
     lax.fori_loop(0, chunks, drain, 0)
@@ -272,11 +499,17 @@
             pltpu.VMEM((rows, 2 * cols), bf16),
             pltpu.VMEM((rows - 3 * tok, 2 * cols), bf16),
             pltpu.VMEM((lines, tok), jnp.float32),
-            pltpu.VMEM((max(8, slots), D_HEAD), jnp.float32),
+            pltpu.VMEM((16, D_HEAD), jnp.float32),
             pltpu.VMEM((tok, 2 * cols), jnp.float32),
             pltpu.VMEM((rows - tok, 2 * cols), bf16),
             pltpu.VMEM((rows - tok, 2 * cols), bf16),
+            pltpu.VMEM((tok, 2 * cols), bf16),
+            pltpu.VMEM((TILE, 2 * cols), bf16),
+            pltpu.VMEM((TILE, 2 * cols), bf16),
+            pltpu.VMEM((tok, 2 * cols), bf16),
             sems, sems, sems, sems,
+            pltpu.SemaphoreType.DMA((4, chunks)),
+            pltpu.SemaphoreType.DMA((3, chunks)),
         ],
         compiler_params=pltpu.CompilerParams(
             collective_id=0, has_side_effects=True, vmem_limit_bytes=60 * 1024 * 1024

time: 186 us -> 158 us (0.85); the launches traced: 186 us -> 156 us
  Pallas kernels: 180 us -> 149 us
    pallas_call x1, Pallas kernels: 180 us -> 149 us  [per_device(): pl.pallas_call(functools.partial(kernel, n, chunk), out_shape=(out,) * 4,...]
where the time goes in v2:
time: 158 us; the launch traced here: 156 us
  Pallas kernels  149 us (94%)
  local copies, waits for them, and re-layouts  5.85 us (4%)
    pallas_call x1, Pallas kernels, per_device(): pl.pallas_call(functools.partial(kernel, n, chunk), out_shape=(out,) * 4,...  149 us
    unnamed x10, local copies, waits for them, and re-layouts  5.85 us

profile of v2, /device:TPU:18, one launch (start us, length us, event | category | flops | bytes accessed | tf_op | source)
XLA Modules:
  0.0 155.5 jit_solution(16292318876865337963)
XLA Ops:
  0.6 149.0 %shard_map.93 = (bf16[256,1536]{1,0:T(8,128)(2,1)}, bf16[256,1536]{1,0:T(8,128)(2,1)}, bf16[256,1536]{1,0:T(8,128)(2,1)}, bf16[256,1536]{1,0:T(8,128)(2,1)}) custom-call(bf16[256,1536]{1,0:T(8,128)(2,1)} %q_ref.1, bf16[256,1536]{1,0:T(8,128)(2,1)} %k_ref.1, bf16[256,1536]{1,0:T(8,128)(2,1)} %v_ref.1, bf16[256,1536]{1,0:T(8,128)(2,1)} %g_ref.1, ...), custom_call_target="tpu_custom_call" | custom-call | flops 7247757312 | bytes 6291456 | tf_op jit(solution)/shard_map/pallas_call | solution.py:493
  149.7 0.0 copy-start.2
  149.7 2.1 %copy.14 = bf16[256,1536]{1,0:T(8,128)(2,1)} copy(bf16[256,1536]{1,0:T(8,128)(2,1)} %get-tuple-element.8) | data formatting | bytes 1572864
  151.8 0.0 copy-done.2
  151.8 0.0 copy-start.1
  151.8 0.9 copy.15
  152.7 0.5 copy-done.1
  153.2 0.0 copy-start
  153.2 0.9 copy.16
  154.1 0.5 copy-done
  154.7 0.9 copy.17
Async XLA Ops:
  149.7 2.1 %copy-start.2 = (bf16[256,1536]{1,0:T(8,128)(2,1)S(1)}, bf16[256,1536]{1,0:T(8,128)(2,1)}, u32[]{:S(2)}) copy-start(bf16[256,1536]{1,0:T(8,128)(2,1)} %get-tuple-element.9) | copy-start | bytes 2359300
  151.8 1.4 copy-start.1
  153.2 1.4 copy-start

commit v3 on v2

--- a/solution.py
+++ b/solution.py
@@ -10,7 +10,7 @@
 
 D_HEAD = 128
 TILE = 128
-LEAD = 3
+LEAD = 12
 MESH = pl.DeviceIdType.MESH
 
 
@@ -26,6 +26,7 @@
 def kernel(
     n, chunk, q_ref, k_ref, v_ref, g_ref, band_ref, far_ref, o_ref, dq_ref, dk_ref, dv_ref,
     kv, picked, bias, marks, own, gsend, grecv, passed, cut, folded, joined,
+    onward, turned, back8, back2, back,
     send_sem, recv_sem, gsend_sem, grecv_sem, xsend_sem, xrecv_sem,
 ):
     tok, cols_all = q_ref.shape
@@ -51,17 +52,21 @@
     cuts = within(pos - side)
     quarter = lax.rem(pos, 4)
     third, zeroth = quarter == 3, quarter == 0
-    ahead = jnp.where(third, 1, -1)
     passer = third | zeroth
-    passes = passer & within(pos - 4 * ahead)
-    starts = passer & within(pos + 4 * ahead)
-    pass_slot = jnp.where(third, 0, 1)
+    upper = quarter >= 2
+    ahead = jnp.where(upper, 1, -1)
+    pass_slot = jnp.where(upper, 0, 1)
+    passes = within(pos - 4 * ahead)
+    starts = within(pos + 4 * ahead)
+    goes_on = passes & starts
     cut_mark, keep_mark = len(far), len(far) + 1
+    on_mark, turn_mark = len(far) + 2, len(far) + 3
+    lower = jnp.logical_not(upper)
     direct = [
-        jnp.logical_not(third), jnp.logical_not(zeroth), odd == 0, odd == 1,
-        jnp.logical_not(third), jnp.logical_not(zeroth),
+        jnp.logical_not(third), jnp.logical_not(zeroth), zeroth, third,
+        lower, upper, lower, upper,
     ]
-    direct += [jnp.bool_(True)] * (len(slots) - 6)
+    direct += [jnp.bool_(True)] * (len(slots) - 8)
 
     def key_out(s):
         return within(pos + slots[s][0]) & direct[s]
@@ -80,7 +85,7 @@
 
     def grad_in(s):
         live = within(pos + slots[s][0])
-        return live if s < 2 else live & direct[s]
+        return live & direct[s]
 
     barrier = pltpu.get_barrier_semaphore()
     partners = jnp.int32(0)
@@ -139,6 +144,32 @@
             xsend_sem.at[0, c], recv_sem.at[pass_slot, c], pos - 3 * ahead,
         )
 
+    def turn_send(c):
+        row = pl.multiple_of(3 * tok + pass_slot * TILE, TILE)
+        return remote(
+            turned.at[:, span(c)], kv.at[pl.ds(row, TILE), span(c)],
+            xsend_sem.at[4, c], recv_sem.at[2 + pass_slot, c], pos - 2 * ahead,
+        )
+
+    def on_send(c):
+        row = pl.multiple_of(3 * tok + (4 + pass_slot) * TILE, TILE)
+        return remote(
+            onward.at[:, span(c)], kv.at[pl.ds(row, TILE), span(c)],
+            xsend_sem.at[5, c], recv_sem.at[6 + pass_slot, c], pos + 4 * ahead,
+        )
+
+    def back2_recv(c):
+        ref = back2.at[:, span(c)]
+        return remote(ref, ref, xsend_sem.at[4, c], xrecv_sem.at[3, c], pos - 2 * ahead)
+
+    def back8_recv(c):
+        ref = back8.at[:, span(c)]
+        return remote(ref, ref, xsend_sem.at[5, c], xrecv_sem.at[4, c], pos + 4 * ahead)
+
+    def back_recv(c):
+        ref = back.at[:, span(c)]
+        return remote(ref, ref, xsend_sem.at[2, c], xrecv_sem.at[5, c], pos + 4 * ahead)
+
     def whole_recv(c):
         ref = kv.at[pl.ds(pl.multiple_of(tok * (1 + odd), tok), tok), span(c)]
         return remote(ref, ref, send_sem.at[odd, c], recv_sem.at[odd, c], pos - side)
@@ -174,10 +205,9 @@
         return remote(ref, ref, xsend_sem.at[2, c], xrecv_sem.at[2, c], pos - 3 * ahead)
 
     def join_send(c):
-        row = pl.multiple_of(tok * pass_slot, tok)
-        return remote(
-            joined.at[:, span(c)], grecv.at[pl.ds(row, tok), span(c)],
-            xsend_sem.at[2, c], grecv_sem.at[pass_slot, c], pos - 4 * ahead,
+        return remote(
+            joined.at[:, span(c)], back.at[:, span(c)],
+            xsend_sem.at[2, c], xrecv_sem.at[5, c], pos - 4 * ahead,
         )
 
     def grad_send(s, c):
@@ -195,21 +225,44 @@
             src, folded.at[:, span(c)], gsend_sem.at[s, c], xrecv_sem.at[1, c], mate
         )
 
+    def turn_back(s, c):
+        d, row, count = slots[s]
+        src = gsend.at[pl.ds(row - tok, count), span(c)]
+        return remote(
+            src, back2.at[:, span(c)], gsend_sem.at[s, c], xrecv_sem.at[3, c], pos + d
+        )
+
+    def on_back(s, c):
+        d, row, count = slots[s]
+        src = gsend.at[pl.ds(row - tok, count), span(c)]
+        return remote(
+            src, back8.at[:, span(c)], gsend_sem.at[s, c], xrecv_sem.at[4, c], pos - d // 2
+        )
+
     def send_grad(s, c, action):
+        never = jnp.bool_(False)
+        to_mate = to_turn = to_on = never
         if s in (2, 3):
             to_mate = odd == 3 - s
+            to_turn = zeroth if s == 2 else third
 
             @pl.when(grad_out(s) & to_mate)
             def _():
                 action(mate_send(s, c))
 
-            @pl.when(grad_out(s) & jnp.logical_not(to_mate))
+            @pl.when(grad_out(s) & to_turn)
             def _():
-                action(grad_send(s, c))
-        else:
-            @pl.when(grad_out(s))
+                action(turn_back(s, c))
+        if s in (6, 7):
+            to_on = upper if s == 6 else lower
+
+            @pl.when(grad_out(s) & to_on)
             def _():
-                action(grad_send(s, c))
+                action(on_back(s, c))
+
+        @pl.when(grad_out(s) & jnp.logical_not(to_mate | to_turn | to_on))
+        def _():
+            action(grad_send(s, c))
 
     def grad_recv(s, c):
         d, row, count = slots[s]
@@ -232,6 +285,12 @@
     )
     marks[pl.ds(keep_mark, 1), :] = jnp.broadcast_to(
         far_entry(pos, pos - 4 * ahead), (1, D_HEAD)
+    )
+    marks[pl.ds(on_mark, 1), :] = jnp.broadcast_to(
+        far_entry(pos + 4 * ahead, pos - 4 * ahead), (1, D_HEAD)
+    )
+    marks[pl.ds(turn_mark, 1), :] = jnp.broadcast_to(
+        far_entry(pos - 2 * ahead, pos - 4 * ahead), (1, D_HEAD)
     )
 
     def pick(ref, j, cols, base=0):
@@ -281,6 +340,14 @@
         @pl.when(jnp.logical_not(within(pos - d)))
         def _():
             kv[pl.ds(row, count), :] = jnp.zeros((count, kv.shape[1]), kv.dtype)
+
+    for ref, filled in (
+        (joined, passes & passer), (back2, passes & jnp.logical_not(passer)),
+        (back8, goes_on), (back, starts),
+    ):
+        @pl.when(jnp.logical_not(filled))
+        def _():
+            ref[...] = jnp.zeros(ref.shape, ref.dtype)
 
     lane = lax.broadcasted_iota(jnp.int32, (1, tok), 1) // TILE
 
@@ -357,13 +424,32 @@
             fold_send(c).start()
 
     def join(c):
+        @pl.when(passes & passer)
+        def _():
+            join_recv(c).wait_recv()
+
+        @pl.when(passes & jnp.logical_not(passer))
+        def _():
+            back2_recv(c).wait_recv()
+
+        @pl.when(goes_on)
+        def _():
+            back8_recv(c).wait_recv()
+
         @pl.when(passes)
         def _():
-            join_recv(c).wait_recv()
             row = pl.multiple_of(2 * tok + (2 + pass_slot) * TILE, TILE)
+            f32 = jnp.float32
             for i in range(2 * chunk):
-                extra = gsend[pl.ds(row, TILE), piece(c, i)].astype(jnp.float32)
-                add_tile(joined, 0, extra, keep_mark, piece(c, i))
+                cols = piece(c, i)
+                kept = gsend[pl.ds(row, TILE), cols].astype(f32)
+                read8, read2 = back8[:, cols].astype(f32), back2[:, cols].astype(f32)
+                for t in range(tiles):
+                    at = pl.ds(t * TILE, TILE)
+                    total = joined[at, cols].astype(f32)
+                    for j, part in ((keep_mark, kept), (on_mark, read8), (turn_mark, read2)):
+                        total = total + (marks[pl.ds(j, 1), :] == float(t)).astype(f32) * part
+                    joined[at, cols] = total.astype(joined.dtype)
             join_send(c).start()
 
     def work(c, carry):
@@ -374,7 +460,25 @@
         @pl.when(passes)
         def _():
             pass_recv(c).wait_recv()
+
+        @pl.when(passes & passer)
+        def _():
             pass_send(c).start()
+
+        @pl.when(goes_on)
+        def _():
+            for i in range(2 * chunk):
+                onward[:, piece(c, i)] = pick(passed, on_mark, piece(c, i))
+            on_send(c).start()
+
+        @pl.when(passes & jnp.logical_not(passer))
+        def _():
+            for i in range(2 * chunk):
+                turned[:, piece(c, i)] = pick(passed, turn_mark, piece(c, i))
+            turn_send(c).start()
+
+        @pl.when(passes)
+        def _():
             row = pl.multiple_of(3 * tok + (2 + pass_slot) * TILE, TILE)
             for i in range(2 * chunk):
                 kv[pl.ds(row, TILE), piece(c, i)] = pick(passed, keep_mark, piece(c, i))
@@ -420,6 +524,10 @@
             @pl.when(grad_in(s))
             def _():
                 grad_recv(s, c).wait_recv()
+
+        @pl.when(starts)
+        def _():
+            back_recv(c).wait_recv()
 
         for i in range(chunk):
             h = c * chunk + i
@@ -428,7 +536,7 @@
                 cols = pl.ds(pl.multiple_of(h * 2 * D_HEAD + part * D_HEAD, D_HEAD), D_HEAD)
                 for t in range(tiles):
                     at = pl.ds(t * TILE, TILE)
-                    total = own[at, cols]
+                    total = own[at, cols] + back[at, cols].astype(jnp.float32)
                     for _, row, _ in slots[:2]:
                         total = total + grecv[pl.ds(row - tok + t * TILE, TILE), cols].astype(
                             jnp.float32
@@ -457,8 +565,19 @@
 
         @pl.when(passes)
         def _():
+            join_send(c).wait_send()
+
+        @pl.when(passes & passer)
+        def _():
             pass_send(c).wait_send()
-            join_send(c).wait_send()
+
+        @pl.when(passes & jnp.logical_not(passer))
+        def _():
+            turn_send(c).wait_send()
+
+        @pl.when(goes_on)
+        def _():
+            on_send(c).wait_send()
 
         @pl.when(cuts)
         def _():
@@ -480,7 +599,7 @@
     tok, cols = queries.shape
     heads = cols // D_HEAD
     n = lax.axis_size("tm")
-    chunk = 2 if heads % 2 == 0 else 1
+    chunk = 3 if heads % 3 == 0 else 1
     chunks = heads // chunk
     slots = 2 + len(far_strides(n))
     rows = 3 * tok + (slots - 2) * TILE
@@ -507,9 +626,14 @@
             pltpu.VMEM((TILE, 2 * cols), bf16),
             pltpu.VMEM((TILE, 2 * cols), bf16),
             pltpu.VMEM((tok, 2 * cols), bf16),
+            pltpu.VMEM((TILE, 2 * cols), bf16),
+            pltpu.VMEM((TILE, 2 * cols), bf16),
+            pltpu.VMEM((TILE, 2 * cols), bf16),
+            pltpu.VMEM((TILE, 2 * cols), bf16),
+            pltpu.VMEM((tok, 2 * cols), bf16),
             sems, sems, sems, sems,
-            pltpu.SemaphoreType.DMA((4, chunks)),
-            pltpu.SemaphoreType.DMA((3, chunks)),
+            pltpu.SemaphoreType.DMA((6, chunks)),
+            pltpu.SemaphoreType.DMA((6, chunks)),
         ],
         compiler_params=pltpu.CompilerParams(
             collective_id=0, has_side_effects=True, vmem_limit_bytes=60 * 1024 * 1024

time: 158 us -> 170 us (1.076)
  Pallas kernels: 149 us -> 163 us
    pallas_call x1, Pallas kernels: 149 us -> 163 us  [per_device(): pl.pallas_call(functools.partial(kernel, n, chunk), out_shape=(out,) * 4,...]
where the time goes in v3:
time: 170 us; the launch traced here: 169 us
  Pallas kernels  163 us (96%)
  local copies, waits for them, and re-layouts  5.85 us (3%)
    pallas_call x1, Pallas kernels, per_device(): pl.pallas_call(functools.partial(kernel, n, chunk), out_shape=(out,) * 4,...  163 us
    unnamed x10, local copies, waits for them, and re-layouts  5.85 us

profile of v3, /device:TPU:18, one launch (start us, length us, event | category | flops | bytes accessed | tf_op | source)
XLA Modules:
  0.0 169.2 jit_solution(4516249371429217761)
XLA Ops:
  0.6 162.7 %shard_map.93 = (bf16[256,1536]{1,0:T(8,128)(2,1)}, bf16[256,1536]{1,0:T(8,128)(2,1)}, bf16[256,1536]{1,0:T(8,128)(2,1)}, bf16[256,1536]{1,0:T(8,128)(2,1)}) custom-call(bf16[256,1536]{1,0:T(8,128)(2,1)} %q_ref.1, bf16[256,1536]{1,0:T(8,128)(2,1)} %k_ref.1, bf16[256,1536]{1,0:T(8,128)(2,1)} %v_ref.1, bf16[256,1536]{1,0:T(8,128)(2,1)} %g_ref.1, ...), custom_call_target="tpu_custom_call" | custom-call | flops 7247757312 | bytes 6291456 | tf_op jit(solution)/shard_map/pallas_call | solution.py:612
  163.3 0.0 copy-start.2
  163.3 2.1 %copy.14 = bf16[256,1536]{1,0:T(8,128)(2,1)} copy(bf16[256,1536]{1,0:T(8,128)(2,1)} %get-tuple-element.8) | data formatting | bytes 1572864
  165.5 0.0 copy-done.2
  165.5 0.0 copy-start.1
  165.5 0.9 copy.15
  166.3 0.5 copy-done.1
  166.9 0.0 copy-start
  166.9 0.9 copy.16
  167.8 0.5 copy-done
  168.3 0.9 copy.17
Async XLA Ops:
  163.3 2.1 %copy-start.2 = (bf16[256,1536]{1,0:T(8,128)(2,1)S(1)}, bf16[256,1536]{1,0:T(8,128)(2,1)}, u32[]{:S(2)}) copy-start(bf16[256,1536]{1,0:T(8,128)(2,1)} %get-tuple-element.9) | copy-start | bytes 2359300
  165.5 1.4 copy-start.1
  166.9 1.4 copy-start

commit v4 on v2

--- a/solution.py
+++ b/solution.py
@@ -10,7 +10,7 @@
 
 D_HEAD = 128
 TILE = 128
-LEAD = 3
+LEAD = 12
 MESH = pl.DeviceIdType.MESH
 
 
@@ -480,7 +480,7 @@
     tok, cols = queries.shape
     heads = cols // D_HEAD
     n = lax.axis_size("tm")
-    chunk = 2 if heads % 2 == 0 else 1
+    chunk = 3 if heads % 3 == 0 else 1
     chunks = heads // chunk
     slots = 2 + len(far_strides(n))
     rows = 3 * tok + (slots - 2) * TILE

time: 158 us -> 155 us (0.981)
  the two profiles are of different devices: /device:TPU:18 before, /device:TPU:7 now
where the time goes in v4:
time: 155 us
  Pallas kernels  148 us (95%)
  local copies, waits for them, and re-layouts  5.85 us (4%)
    pallas_call x1, Pallas kernels, per_device(): pl.pallas_call(functools.partial(kernel, n, chunk), out_shape=(out,) * 4,...  148 us
    unnamed x10, local copies, waits for them, and re-layouts  5.85 us

profile of v4, /device:TPU:7, one launch (start us, length us, event | category | flops | bytes accessed | tf_op | source)
XLA Modules:
  0.0 154.6 jit_solution(2537471870870390729)
XLA Ops:
  0.6 148.1 %shard_map.93 = (bf16[256,1536]{1,0:T(8,128)(2,1)}, bf16[256,1536]{1,0:T(8,128)(2,1)}, bf16[256,1536]{1,0:T(8,128)(2,1)}, bf16[256,1536]{1,0:T(8,128)(2,1)}) custom-call(bf16[256,1536]{1,0:T(8,128)(2,1)} %q_ref.1, bf16[256,1536]{1,0:T(8,128)(2,1)} %k_ref.1, bf16[256,1536]{1,0:T(8,128)(2,1)} %v_ref.1, bf16[256,1536]{1,0:T(8,128)(2,1)} %g_ref.1, ...), custom_call_target="tpu_custom_call" | custom-call | flops 7247757312 | bytes 6291456 | tf_op jit(solution)/shard_map/pallas_call | solution.py:493
  148.8 0.0 copy-start.2
  148.8 2.1 %copy.14 = bf16[256,1536]{1,0:T(8,128)(2,1)} copy(bf16[256,1536]{1,0:T(8,128)(2,1)} %get-tuple-element.8) | data formatting | bytes 1572864
  150.9 0.0 copy-done.2
  150.9 0.0 copy-start.1
  150.9 0.9 copy.15
  151.8 0.5 copy-done.1
  152.3 0.0 copy-start
  152.3 0.9 copy.16
  153.2 0.5 copy-done
  153.7 0.9 copy.17
Async XLA Ops:
  148.8 2.1 %copy-start.2 = (bf16[256,1536]{1,0:T(8,128)(2,1)S(1)}, bf16[256,1536]{1,0:T(8,128)(2,1)}, u32[]{:S(2)}) copy-start(bf16[256,1536]{1,0:T(8,128)(2,1)} %get-tuple-element.9) | copy-start | bytes 2359300
  150.9 1.4 copy-start.1
  152.3 1.4 copy-start
